TPU v7x, 32 devices: a whole 2x2x4 slice. The times are simulated.
32 devices in a mesh: section: 2 (over x), dp: 16 (over z, y, core).
Axes of the slice: x: 2, y: 2, z: 4, core: 2. Of those that a mesh axis runs over, the one named last changes fastest.
Arguments:
- hidden_in: bfloat16 [2, 16, 512, 768], P(None, 'dp'), may hold values from -6 to 6
- seg_ids: int32 [2, 16, 512], P(None, 'dp'), may hold values from 0 to 3, never falling along the last dimension, each value on 1 to 256 neighbouring positions
- pair_ids: int32 [2, 64], P(None, 'dp'), may hold values from 0 to 63, as said below
- w_qkv: bfloat16 [2, 768, 2304], P('section'), may hold values from -0.21875 to 0.21875
- b_query: bfloat16 [2, 768], P('section'), may hold values from -3 to 3
- b_value: bfloat16 [2, 768], P('section'), may hold values from -3 to 3
- w_attn_out: bfloat16 [2, 768, 768], P('section'), may hold values from -0.875 to 0.875
- b_attn_out: bfloat16 [2, 768], P('section'), may hold values from -1.75 to 1.75
- ln1_gain: bfloat16 [2, 768], P('section'), may hold values from 0.5 to 1.5
- ln1_bias: bfloat16 [2, 768], P('section'), may hold values from -1.75 to 1.75
- w_in: bfloat16 [2, 768, 3072], P('section'), may hold values from -0.21875 to 0.21875
- b_in: bfloat16 [2, 3072], P('section'), may hold values from -3 to 3
- w_out: bfloat16 [2, 3072, 768], P('section'), may hold values from -0.109375 to 0.109375
- b_out: bfloat16 [2, 768], P('section'), may hold values from -1.75 to 1.75
- ln2_gain: bfloat16 [2, 768], P('section'), may hold values from 0.5 to 1.5
- ln2_bias: bfloat16 [2, 768], P('section'), may hold values from -0.625 to 0.625
Outputs:
- pooled: float32 [2, 64, 768], P(None, 'dp', 'section')
- seg_loss: float32 [2, 64], P(None, 'dp')
- grad_input: float32 [2, 16, 512, 768], P(None, 'dp', None, 'section')
- grad_w_qkv: float32 [2, 768, 2304], P('section', 'dp')
- grad_b_query: float32 [2, 768], P('section', 'dp')
- grad_b_value: float32 [2, 768], P('section', 'dp')
- grad_w_attn_out: float32 [2, 768, 768], P('section', 'dp')
- grad_b_attn_out: float32 [2, 768], P('section', 'dp')
- grad_ln1_gain: float32 [2, 768], P('section', 'dp')
- grad_ln1_bias: float32 [2, 768], P('section', 'dp')
- grad_w_in: float32 [2, 768, 3072], P('section', 'dp')
- grad_b_in: float32 [2, 3072], P('section', 'dp')
- grad_w_out: float32 [2, 3072, 768], P('section', 'dp')
- grad_b_out: float32 [2, 768], P('section', 'dp')
- grad_ln2_gain: float32 [2, 768], P('section', 'dp')
- grad_ln2_bias: float32 [2, 768], P('section', 'dp')
Inputs may be any that keep to these rules, and one draw needn't show every extreme that they name: `seg_ids`: in each row the document numbers never fall and all 4 of them occur. In each micro-batch pair_ids is a permutation of the 64 documents forming one cycle; no document is its own partner.
All inputs are finite; a program needn't handle non-finite values.
Results may differ from a plain program's by a relative error of at most 0.02.
Values may be sent and summed in bfloat16 or wider, within the bound.
A program may use at most 256 MiB of HBM per device.

v0:
```python
import jax
import jax.numpy as jnp
from jax import lax
from jax.sharding import PartitionSpec as P

HEADS = 12
SEGS = 4


MASK_FILL = 1000000000.0
NORM_EPS = 1e-12
UNIT_EPS = 1e-06
TEMPER = 20.0
HIGHEST = lax.Precision.HIGHEST


def passed_along(value, axis, steps):
    count = lax.axis_size(axis)
    initial, last = (max(0, -steps), min(count, count - steps))
    return lax.ppermute(value, axis, [(source, source + steps) for source in range(initial, last)])


def swapped(value, axis, stride):
    mask = 2**stride
    pairs = [(source, source ^ mask) for source in range(lax.axis_size(axis))]
    return lax.ppermute(value, axis, pairs)


def layer_norm(row_values, gain, shift):
    centre = row_values - jnp.mean(row_values, axis=-1, keepdims=True)
    scaling = lax.rsqrt(jnp.mean(centre * centre, axis=-1, keepdims=True) + NORM_EPS)
    normed = centre * scaling
    return (normed * gain + shift, normed, scaling)


def norm_back(normed, scaling, gain, upstream):
    scaled = upstream * gain
    downstream = scaling * (
        scaled
        - jnp.mean(scaled, axis=-1, keepdims=True)
        - normed * jnp.mean(scaled * normed, axis=-1, keepdims=True)
    )
    return (downstream, jnp.sum(upstream * normed, axis=0), jnp.sum(upstream, axis=0))


def contract_rows(left, right):
    return lax.dot_general(
        left, right, (((0,), (0,)), ((), ())), preferred_element_type=jnp.float32
    )


def masked_scores(queries, key_rows, segments):
    scaling = queries.shape[-1] ** (-0.5)
    scores = (
        jnp.einsum("qhd,khd->hqk", queries, key_rows, preferred_element_type=jnp.float32) * scaling
    )
    same_segment = segments[:, None] == segments[None, :]
    return (jnp.where(same_segment[None], scores, -MASK_FILL), scaling)


def attend_row(row_items):
    queries, key_rows, values, segments = row_items
    scores, scaling = masked_scores(queries, key_rows, segments)
    peak_value = jnp.max(scores, axis=-1, keepdims=True)
    exponent = jnp.exp(scores - peak_value)
    denominator = jnp.sum(exponent, axis=-1, keepdims=True)
    weights_low = (exponent / denominator).astype(jnp.bfloat16)
    context = jnp.einsum("hqk,khd->qhd", weights_low, values, preferred_element_type=jnp.float32)
    return (context.astype(jnp.bfloat16), (peak_value + jnp.log(denominator))[..., 0])


def attend_back(row_items):
    queries, key_rows, values, segments, log_totals, d_context = row_items
    scores, scaling = masked_scores(queries, key_rows, segments)
    weights_full = jnp.exp(scores - log_totals[..., None])
    weights_low = weights_full.astype(jnp.bfloat16)
    d_values = jnp.einsum(
        "hqk,qhd->khd", weights_low, d_context, preferred_element_type=jnp.float32
    )
    d_weights = jnp.einsum("qhd,khd->hqk", d_context, values, preferred_element_type=jnp.float32)
    inner_sum = jnp.sum(weights_full * d_weights, axis=-1, keepdims=True)
    d_scores = (weights_full * (d_weights - inner_sum)).astype(jnp.bfloat16)
    d_queries = (
        jnp.einsum("hqk,khd->qhd", d_scores, key_rows, preferred_element_type=jnp.float32) * scaling
    )
    d_keys = (
        jnp.einsum("hqk,qhd->khd", d_scores, queries, preferred_element_type=jnp.float32) * scaling
    )
    return (
        d_queries.astype(jnp.bfloat16),
        d_keys.astype(jnp.bfloat16),
        d_values.astype(jnp.bfloat16),
    )


def layer_forward(inputs, segments, weight_set):
    (
        w_qkv,
        b_query,
        b_value,
        w_attn,
        b_attn,
        gain_one,
        bias_one,
        w_in,
        b_in,
        w_out,
        b_out,
        gain_two,
        bias_two,
    ) = weight_set
    row_count, seq_len, feature_width = inputs.shape
    token_count = row_count * seq_len
    head_shape = (row_count, seq_len, HEADS, feature_width // HEADS)
    flat_inputs = inputs.reshape(token_count, feature_width)
    projected = jnp.dot(flat_inputs, w_qkv, preferred_element_type=jnp.float32)
    queries = (projected[:, :feature_width] + b_query).astype(jnp.bfloat16)
    key_rows = projected[:, feature_width : 2 * feature_width].astype(jnp.bfloat16)
    values = (projected[:, 2 * feature_width :] + b_value).astype(jnp.bfloat16)
    context, log_totals = lax.map(
        attend_row,
        (
            queries.reshape(head_shape),
            key_rows.reshape(head_shape),
            values.reshape(head_shape),
            segments,
        ),
    )
    context = context.reshape(token_count, feature_width)
    first_sum = (
        flat_inputs.astype(jnp.float32)
        + jnp.dot(context, w_attn, preferred_element_type=jnp.float32)
        + b_attn
    )
    hidden, normed_one, scale_one = layer_norm(first_sum, gain_one, bias_one)
    hidden_low = hidden.astype(jnp.bfloat16)
    pre_act = jnp.dot(hidden_low, w_in, preferred_element_type=jnp.float32) + b_in
    active = jax.nn.gelu(pre_act, approximate=False).astype(jnp.bfloat16)
    second_sum = hidden + jnp.dot(active, w_out, preferred_element_type=jnp.float32) + b_out
    output, normed_two, scale_two = layer_norm(second_sum, gain_two, bias_two)
    stash = (
        flat_inputs,
        queries,
        key_rows,
        values,
        log_totals,
        context,
        normed_one,
        scale_one,
        hidden_low,
        pre_act,
        active,
        normed_two,
        scale_two,
        segments,
    )
    return (output.reshape(row_count, seq_len, feature_width), stash)


def layer_back_input(stash, upstream, weight_set):
    (
        w_qkv,
        b_query,
        b_value,
        w_attn,
        b_attn,
        gain_one,
        bias_one,
        w_in,
        b_in,
        w_out,
        b_out,
        gain_two,
        bias_two,
    ) = weight_set
    (
        flat_inputs,
        queries,
        key_rows,
        values,
        log_totals,
        context,
        normed_one,
        scale_one,
        hidden_low,
        pre_act,
        active,
        normed_two,
        scale_two,
        segments,
    ) = stash
    row_count, seq_len = segments.shape
    token_count, feature_width = flat_inputs.shape
    head_shape = (row_count, seq_len, HEADS, feature_width // HEADS)
    d_second, grad_gain_two, grad_bias_two = norm_back(normed_two, scale_two, gain_two, upstream)
    d_branch_two = d_second.astype(jnp.bfloat16)
    d_active = jnp.dot(d_branch_two, w_out.T, preferred_element_type=jnp.float32)
    gelu_pull = jax.vjp(lambda value_in: jax.nn.gelu(value_in, approximate=False), pre_act)[1]
    d_pre = gelu_pull(d_active)[0].astype(jnp.bfloat16)
    d_hidden = d_second + jnp.dot(d_pre, w_in.T, preferred_element_type=jnp.float32)
    d_first, grad_gain_one, grad_bias_one = norm_back(normed_one, scale_one, gain_one, d_hidden)
    d_branch_one = d_first.astype(jnp.bfloat16)
    d_context = jnp.dot(d_branch_one, w_attn.T, preferred_element_type=jnp.float32).astype(
        jnp.bfloat16
    )
    d_queries, d_keys, d_values = lax.map(
        attend_back,
        (
            queries.reshape(head_shape),
            key_rows.reshape(head_shape),
            values.reshape(head_shape),
            segments,
            log_totals,
            d_context.reshape(head_shape),
        ),
    )
    d_projected = jnp.concatenate(
        [
            d_queries.reshape(token_count, feature_width),
            d_keys.reshape(token_count, feature_width),
            d_values.reshape(token_count, feature_width),
        ],
        axis=1,
    )
    d_inputs = d_first + jnp.dot(d_projected, w_qkv.T, preferred_element_type=jnp.float32)
    back_parts = (
        d_branch_two,
        d_pre,
        d_branch_one,
        d_projected,
        grad_gain_one,
        grad_bias_one,
        grad_gain_two,
        grad_bias_two,
    )
    return (d_inputs, back_parts)


def layer_back_weights(stash, back_parts):
    (
        flat_inputs,
        queries,
        key_rows,
        values,
        log_totals,
        context,
        normed_one,
        scale_one,
        hidden_low,
        pre_act,
        active,
        normed_two,
        scale_two,
        segments,
    ) = stash
    (
        d_branch_two,
        d_pre,
        d_branch_one,
        d_projected,
        grad_gain_one,
        grad_bias_one,
        grad_gain_two,
        grad_bias_two,
    ) = back_parts
    feature_width = flat_inputs.shape[1]
    grad_qkv = contract_rows(flat_inputs, d_projected)
    grad_query_bias = jnp.sum(d_projected[:, :feature_width].astype(jnp.float32), axis=0)
    grad_value_bias = jnp.sum(d_projected[:, 2 * feature_width :].astype(jnp.float32), axis=0)
    grad_attn = contract_rows(context, d_branch_one)
    grad_attn_bias = jnp.sum(d_branch_one.astype(jnp.float32), axis=0)
    grad_in = contract_rows(hidden_low, d_pre)
    grad_in_bias = jnp.sum(d_pre.astype(jnp.float32), axis=0)
    grad_out = contract_rows(active, d_branch_two)
    grad_out_bias = jnp.sum(d_branch_two.astype(jnp.float32), axis=0)
    return (
        grad_qkv,
        grad_query_bias,
        grad_value_bias,
        grad_attn,
        grad_attn_bias,
        grad_gain_one,
        grad_bias_one,
        grad_in,
        grad_in_bias,
        grad_out,
        grad_out_bias,
        grad_gain_two,
        grad_bias_two,
    )


def score_grads(unit_rows, all_units, row_start, partners):
    row_total = unit_rows.shape[0]
    logits = TEMPER * lax.dot_general(
        unit_rows, all_units, (((1,), (1,)), ((), ())), preferred_element_type=jnp.float32
    )
    columns = jnp.arange(all_units.shape[0])
    row_numbers = row_start + jnp.arange(row_total)
    logits = jnp.where(columns[None, :] == row_numbers[:, None], -MASK_FILL, logits)
    peak_value = jnp.max(logits, axis=-1, keepdims=True)
    exponent = jnp.exp(logits - peak_value)
    denominator = jnp.sum(exponent, axis=-1, keepdims=True)
    target_mask = columns[None, :] == partners[:, None]
    seg_losses = (
        peak_value[:, 0]
        + jnp.log(denominator[:, 0])
        - jnp.sum(jnp.where(target_mask, logits, 0.0), axis=-1)
    )
    d_logits = (exponent / denominator - target_mask.astype(jnp.float32)).astype(jnp.bfloat16)
    return (seg_losses, d_logits)


def contrast_head(output, segments, pairs):
    row_count, seq_len, feature_width = output.shape
    member_mask = (segments[:, :, None] == jnp.arange(SEGS)[None, None, :]).astype(jnp.float32)
    seg_sums = jnp.einsum(
        "rsj,rsd->rjd", member_mask, output, precision=HIGHEST, preferred_element_type=jnp.float32
    )
    counts = jnp.sum(member_mask, axis=1)
    pooled = (seg_sums / counts[:, :, None]).reshape(row_count * SEGS, feature_width)
    radius = lax.rsqrt(jnp.sum(pooled * pooled, axis=-1, keepdims=True) + UNIT_EPS)
    unit_low = (pooled * radius).astype(jnp.bfloat16)
    local_count = unit_low.shape[0]
    all_units, all_pairs = (
        lax.all_gather(unit_low, "dp", axis=0, tiled=True),
        lax.all_gather(pairs, "dp", axis=0, tiled=True),
    )
    own_start = lax.axis_index("dp") * local_count
    seg_losses, d_logits = score_grads(unit_low, all_units, own_start, pairs)
    row_term = jnp.dot(d_logits, all_units, preferred_element_type=jnp.float32)
    all_scores = lax.all_gather(d_logits, "dp", axis=0, tiled=True)
    own_columns = lax.dynamic_slice_in_dim(all_scores, own_start, local_count, 1)
    column_term = contract_rows(own_columns, all_units)
    d_unit = TEMPER * (row_term + column_term)
    d_pooled = (
        radius * d_unit
        - radius * radius * radius * jnp.sum(pooled * d_unit, axis=-1, keepdims=True) * pooled
    )
    spread = (d_pooled / counts.reshape(-1)[:, None]).reshape(row_count, SEGS, feature_width)
    d_output = jnp.einsum(
        "rsj,rjd->rsd", member_mask, spread, precision=HIGHEST, preferred_element_type=jnp.float32
    )
    return (pooled, seg_losses, d_output)


def local(
    hidden_in,
    seg_ids,
    pair_ids,
    w_qkv,
    b_query,
    b_value,
    w_attn_out,
    b_attn_out,
    ln1_gain,
    ln1_bias,
    w_in,
    b_in,
    w_out,
    b_out,
    ln2_gain,
    ln2_bias,
):
    weight_set = tuple(
        (
            weight_arg[0]
            for weight_arg in (
                w_qkv,
                b_query,
                b_value,
                w_attn_out,
                b_attn_out,
                ln1_gain,
                ln1_bias,
                w_in,
                b_in,
                w_out,
                b_out,
                ln2_gain,
                ln2_bias,
            )
        )
    )
    micro_count, row_count, seq_len, feature_width = hidden_in.shape
    token_count = row_count * seq_len
    section_index = lax.axis_index("section")
    first_section = section_index == 0
    incoming = jnp.zeros(hidden_in.shape[1:], jnp.bfloat16)
    stash_list = []
    upstream_list = []
    pooled_list = []
    loss_list = []
    for step_index in range(micro_count + 1):
        front_micro = min(step_index, micro_count - 1)
        back_micro = max(step_index - 1, 0)
        inputs = jnp.where(first_section, hidden_in[front_micro], incoming)
        segments = jnp.where(first_section, seg_ids[front_micro], seg_ids[back_micro])
        output, stash = layer_forward(inputs, segments, weight_set)
        stash_list.append(stash)
        if step_index < micro_count:
            incoming = passed_along(output.astype(jnp.bfloat16), "section", 1)
        if step_index >= 1:
            pooled, seg_losses, d_output = contrast_head(output, segments, pair_ids[step_index - 1])
            pooled_list.append(pooled)
            loss_list.append(seg_losses)
            upstream_list.append(d_output.reshape(token_count, feature_width))
    stacked = jax.tree.map(lambda *leaves: jnp.stack(leaves), *stash_list)
    returned = jnp.zeros(hidden_in.shape[1:], jnp.bfloat16)
    input_grads = []
    totals = None
    for step_index in range(micro_count + 1):
        stash_index = jnp.clip(
            jnp.where(first_section, step_index - 1, step_index + 1), 0, micro_count
        )
        stash = jax.tree.map(
            lambda leaf_value: lax.dynamic_index_in_dim(leaf_value, stash_index, 0, keepdims=False),
            stacked,
        )
        upstream = jnp.where(
            first_section,
            returned.reshape(token_count, feature_width).astype(jnp.float32),
            upstream_list[min(step_index, micro_count - 1)],
        )
        d_inputs, back_parts = layer_back_input(stash, upstream, weight_set)
        if step_index < micro_count:
            returned = passed_along(
                d_inputs.astype(jnp.bfloat16).reshape(row_count, seq_len, feature_width),
                "section",
                -1,
            )
        if step_index >= 1:
            input_grads.append(d_inputs.reshape(row_count, seq_len, feature_width))
        live_mask = jnp.where(first_section, step_index >= 1, step_index < micro_count).astype(
            jnp.float32
        )
        weight_grads = tuple(
            (live_mask * grad_part for grad_part in layer_back_weights(stash, back_parts))
        )
        totals = (
            weight_grads
            if totals is None
            else tuple(
                (earlier_sum + fresh_sum for earlier_sum, fresh_sum in zip(totals, weight_grads))
            )
        )
    totals = lax.psum_scatter(
        tuple((grad_part[None] for grad_part in totals)), "dp", scatter_dimension=1, tiled=True
    )
    half_width = feature_width // 2
    keep_start = section_index * half_width
    send_start = (1 - section_index) * half_width
    grad_all = jnp.stack(input_grads)
    pooled_all = jnp.stack(pooled_list)
    loss_all = jnp.stack(loss_list)
    arrived = (
        swapped(
            lax.dynamic_slice_in_dim(grad_all, send_start, half_width, 3).astype(jnp.bfloat16),
            "section",
            0,
        ).astype(jnp.float32),
        swapped(
            lax.dynamic_slice_in_dim(pooled_all, send_start, half_width, 2).astype(jnp.bfloat16),
            "section",
            0,
        ).astype(jnp.float32),
        swapped(loss_all.astype(jnp.bfloat16), "section", 0).astype(loss_all.dtype),
    )
    grad_input = jnp.where(
        first_section, lax.dynamic_slice_in_dim(grad_all, keep_start, half_width, 3), arrived[0]
    )
    pooled_out = jnp.where(
        first_section, arrived[1], lax.dynamic_slice_in_dim(pooled_all, keep_start, half_width, 2)
    )
    loss_out = jnp.where(first_section, arrived[2], loss_all)
    return (
        pooled_out,
        loss_out,
        grad_input,
        totals[0],
        totals[1],
        totals[2],
        totals[3],
        totals[4],
        totals[5],
        totals[6],
        totals[7],
        totals[8],
        totals[9],
        totals[10],
        totals[11],
        totals[12],
    )


def solution(mesh):
    in_specs = (
        P(None, "dp", None, None),
        P(None, "dp", None),
        P(None, "dp"),
        P("section", None, None),
        P("section", None),
        P("section", None),
        P("section", None, None),
        P("section", None),
        P("section", None),
        P("section", None),
        P("section", None, None),
        P("section", None),
        P("section", None, None),
        P("section", None),
        P("section", None),
        P("section", None),
    )
    out_specs = (
        P(None, "dp", "section"),
        P(None, "dp"),
        P(None, "dp", None, "section"),
        P("section", "dp", None),
        P("section", "dp"),
        P("section", "dp"),
        P("section", "dp", None),
        P("section", "dp"),
        P("section", "dp"),
        P("section", "dp"),
        P("section", "dp", None),
        P("section", "dp"),
        P("section", "dp", None),
        P("section", "dp"),
        P("section", "dp"),
        P("section", "dp"),
    )
    return jax.shard_map(local, mesh=mesh, in_specs=in_specs, out_specs=out_specs, check_vma=False)
```

profile of v0, /device:TPU:0, one launch (start us, length us, event | category | flops | bytes accessed | tf_op | source)
XLA Modules:
  0.0 1511.4 jit_solution(295076051080898427)
XLA Ops:
  33.9 5.1 fusion.238
  40.5 20.3 %add_bitcast_fusion.5 = (f32[1,512,3072]{2,1,0:T(8,128)}, bf16[512,3072]{1,0:T(8,128)(2,1)S(1)}) fusion(f32[3072]{0:T(1024)S(1)} %bitcast.840, bf16[1,768,3072]{2,1,0:T(8,128)(2,1)} %param.26, f32[512,768]{1,0:T(8,128)S(1)} %get-tuple-element.270, f32[768]{0:T(1024)S(1)} %get-tuple-element.328, f32[768]{0:T(1024)S(1)} %get-tuple-element.329, ...), kind=kOutput, calls=%fused_computation.196 | convolution fusion | flops 2521694208 | bytes 15751168 | tf_op jit(solution)/shard_map/dot_general | solution.py:137
  66.0 5.7 collective-permute-start
  108.8 5.1 fusion.237
  115.3 20.2 %add_bitcast_fusion.4 = (f32[1,512,3072]{2,1,0:T(8,128)}, bf16[512,3072]{1,0:T(8,128)(2,1)S(1)}) fusion(f32[3072]{0:T(1024)S(1)} %bitcast.841, bf16[1,768,3072]{2,1,0:T(8,128)(2,1)} %param.26, f32[512,768]{1,0:T(8,128)S(1)} %get-tuple-element.276, f32[512]{0:T(512)S(1)} %add_rsqrt_fusion.3, f32[512]{0:T(512)S(1)} %broadcast_multiply_fusion.15, ...), kind=kOutput, calls=%fused_computation.195 | convolution fusion | flops 2521694208 | bytes 15751168 | tf_op jit(solution)/shard_map/dot_general | solution.py:137
  141.6 5.5 collective-permute-start.1
  147.7 23.3 %all-gather = bf16[16,4,768]{2,1,0:T(4,128)(2,1)} all-gather(bf16[1,4,768]{2,1,0:T(4,128)(2,1)S(1)} %fusion.396), channel_id=1, replica_groups=mesh['section'=2,'dp'=16] {'dp'}, dimensions={0}, use_global_device_ids=true | all-gather | bytes 104448 | tf_op jit(solution)/shard_map/all_gather | solution.py:326
  175.8 17.4 %all-gather.2 = bf16[16,4,64]{2,1,0:T(4,128)(2,1)S(1)} all-gather(bf16[1,4,64]{2,1,0:T(4,128)(2,1)S(1)} %fusion.490), channel_id=1, replica_groups=mesh['section'=2,'dp'=16] {'dp'}, dimensions={0}, use_global_device_ids=true | all-gather | bytes 8704 | tf_op jit(solution)/shard_map/all_gather | solution.py:332
  222.0 5.3 fusion.236
  228.8 19.4 %add_bitcast_fusion.3 = (f32[1,512,3072]{2,1,0:T(8,128)}, bf16[512,3072]{1,0:T(8,128)(2,1)S(1)}) fusion(f32[3072]{0:T(1024)S(1)} %bitcast.842, bf16[1,768,3072]{2,1,0:T(8,128)(2,1)} %param.26, f32[512,768]{1,0:T(8,128)S(1)} %get-tuple-element.282, f32[512]{0:T(512)S(1)} %add_rsqrt_fusion.1, f32[512]{0:T(512)S(1)} %broadcast_multiply_fusion.13, ...), kind=kOutput, calls=%fused_computation.194 | convolution fusion | flops 2521694208 | bytes 15751168 | tf_op jit(solution)/shard_map/dot_general | solution.py:137
  262.3 6.1 pad_maximum_fusion
  269.8 19.7 %convert_reduce_fusion.2 = (f32[3072]{0:T(1024)}, bf16[512,3072]{1,0:T(8,128)(2,1)S(1)}) fusion(bf16[1,3072,768]{2,1,0:T(8,128)(2,1)} %param.28, f32[512,768]{1,0:T(8,128)S(1)} %get-tuple-element.188, f32[3,512,3072]{2,1,0:T(8,128)S(1)} %pad_maximum_fusion, s32[]{:T(128)S(6)} %min.11), kind=kOutput, calls=%fused_computation.94 | convolution fusion | flops 2532701184 | bytes 15740932 | tf_op jit(solution)/shard_map/dot_general | solution.py:197
  289.8 4.7 slice-done.28
  326.6 4.6 convert_reduce_fusion.11
  331.2 6.8 multiply_reduce_fusion.2
  338.0 7.4 multiply_convert_fusion.2
  352.6 20.4 %all-gather.1 = bf16[16,4,768]{2,1,0:T(4,128)(2,1)} all-gather(bf16[1,4,768]{2,1,0:T(4,128)(2,1)S(1)} %fusion.397), channel_id=1, replica_groups=mesh['section'=2,'dp'=16] {'dp'}, dimensions={0}, use_global_device_ids=true | all-gather | bytes 104448 | tf_op jit(solution)/shard_map/all_gather | solution.py:326
  375.8 5.1 fusion.240
  383.0 17.4 %all-gather.3 = bf16[16,4,64]{2,1,0:T(4,128)(2,1)S(1)} all-gather(bf16[1,4,64]{2,1,0:T(4,128)(2,1)S(1)} %fusion.489), channel_id=1, replica_groups=mesh['section'=2,'dp'=16] {'dp'}, dimensions={0}, use_global_device_ids=true | all-gather | bytes 8704 | tf_op jit(solution)/shard_map/all_gather | solution.py:332
  423.4 6.4 fusion.431
  435.2 20.1 %convert_reduce_fusion.1 = (f32[3072]{0:T(1024)}, bf16[512,3072]{1,0:T(8,128)(2,1)S(1)}) fusion(bf16[1,3072,768]{2,1,0:T(8,128)(2,1)S(1)} %bitcast.856, f32[512,768]{1,0:T(8,128)S(1)} %get-tuple-element.190, f32[3,512,3072]{2,1,0:T(8,128)} %copy-done.4, s32[]{:T(128)S(6)} %min.10), kind=kOutput, calls=%fused_computation.93 | convolution fusion | flops 2532701184 | bytes 15740932 | tf_op jit(solution)/shard_map/dot_general | solution.py:197
  465.2 8.7 convert_reduce_fusion.10
  474.0 11.2 multiply_reduce_fusion.1
  486.8 7.2 multiply_convert_fusion.1
  501.3 7.2 fusion.432
  512.0 10.8 collective-permute-done.5
  525.0 20.4 %convert_reduce_fusion = (f32[3072]{0:T(1024)}, bf16[512,3072]{1,0:T(8,128)(2,1)S(1)}) fusion(bf16[1,3072,768]{2,1,0:T(8,128)(2,1)S(1)} %bitcast.858, f32[512,768]{1,0:T(8,128)S(1)} %get-tuple-element.192, f32[3,512,3072]{2,1,0:T(8,128)} %copy-done.4, s32[]{:T(128)S(6)} %min.12), kind=kOutput, calls=%fused_computation.92 | convolution fusion | flops 2532701184 | bytes 15740932 | tf_op jit(solution)/shard_map/dot_general | solution.py:197
  555.2 9.5 convert_reduce_fusion.9
  564.8 11.0 multiply_reduce_fusion
  577.4 7.2 multiply_convert_fusion
  603.3 5.4 add_bitcast_fusion.6
  619.1 7.1 add_bitcast_fusion.2
  634.3 9.6 add_bitcast_fusion.1
  644.0 5.6 pad_maximum_fusion.1
  653.4 5.1 fusion.160
  658.5 11.7 add_bitcast_fusion
  679.0 17.5 %collective-permute-done.3 = bf16[2,4]{1,0:T(2,128)(2,1)S(1)} collective-permute-done((bf16[2,4]{1,0:T(2,128)(2,1)S(1)}, bf16[2,4]{1,0:T(2,128)(2,1)S(1)}, u32[]{:S(2)}, u32[]{:S(2)}) %collective-permute-start.3) | collective-permute-done | bytes 48 | tf_op jit(solution)/shard_map/ppermute | solution.py:26
  701.8 56.8 %reduce-scatter.44.cloned.1.call-done = f32[48,1]{1,0:T(8,128)} async-done(((f32[768,1]{1,0:T(8,128)}), f32[48,1]{1,0:T(8,128)}) %reduce-scatter.44.cloned.1.call-update) | async-done | bytes 208
  759.9 57.1 %reduce-scatter.46.cloned.1.call-done = f32[48,1]{1,0:T(8,128)} async-done(((f32[768,1]{1,0:T(8,128)}), f32[48,1]{1,0:T(8,128)}) %reduce-scatter.46.cloned.1.call-update) | async-done | bytes 208
  818.3 56.6 %reduce-scatter.48.cloned.1.call-done = f32[48,1]{1,0:T(8,128)} async-done(((f32[768,1]{1,0:T(8,128)}), f32[48,1]{1,0:T(8,128)}) %reduce-scatter.48.cloned.1.call-update) | async-done | bytes 208
  876.3 57.1 %reduce-scatter.52.cloned.1.call-done = f32[48,1]{1,0:T(8,128)} async-done(((f32[768,1]{1,0:T(8,128)}), f32[48,1]{1,0:T(8,128)}) %reduce-scatter.52.cloned.1.call-update) | async-done | bytes 208
  934.7 56.7 %reduce-scatter.54.cloned.1.call-done = f32[48,1]{1,0:T(8,128)} async-done(((f32[768,1]{1,0:T(8,128)}), f32[48,1]{1,0:T(8,128)}) %reduce-scatter.54.cloned.1.call-update) | async-done | bytes 208
  992.8 57.2 %reduce-scatter.56.cloned.1.call-done = f32[48,1]{1,0:T(8,128)} async-done(((f32[768,1]{1,0:T(8,128)}), f32[48,1]{1,0:T(8,128)}) %reduce-scatter.56.cloned.1.call-update) | async-done | bytes 208
  1051.4 60.9 %reduce-scatter.50.cloned.1.call-done = f32[192,1]{1,0:T(8,128)} async-done(((f32[3072,1]{1,0:T(8,128)}), f32[192,1]{1,0:T(8,128)}) %reduce-scatter.50.cloned.1.call-update) | async-done | bytes 784
  1116.7 62.2 %reduce-scatter.34.cloned.1.call-done = f32[1,48,768]{2,1,0:T(8,128)} async-done(((f32[1,768,768]{2,1,0:T(8,128)}), f32[1,48,768]{2,1,0:T(8,128)}) %reduce-scatter.34.cloned.1.call-update) | async-done | bytes 147472 | tf_op jit(solution)/shard_map/reduce_scatter | solution.py:447
  1178.9 93.7 %reduce-scatter.32.cloned.1.call-done = f32[1,48,2304]{2,1,0:T(8,128)} async-done(((f32[1,768,2304]{2,1,0:T(8,128)}), f32[1,48,2304]{2,1,0:T(8,128)}) %reduce-scatter.32.cloned.1.call-update) | async-done | bytes 442384 | tf_op jit(solution)/shard_map/reduce_scatter | solution.py:447
  1272.6 116.0 %reduce-scatter.36.cloned.1.call-done = f32[1,48,3072]{2,1,0:T(8,128)} async-done(((f32[1,768,3072]{2,1,0:T(8,128)}), f32[1,48,3072]{2,1,0:T(8,128)}) %reduce-scatter.36.cloned.1.call-update) | async-done | bytes 589840 | tf_op jit(solution)/shard_map/reduce_scatter | solution.py:447
  1388.6 115.8 %reduce-scatter.38.cloned.1.call-done = f32[1,192,768]{2,1,0:T(8,128)} async-done(((f32[1,3072,768]{2,1,0:T(8,128)}), f32[1,192,768]{2,1,0:T(8,128)}) %reduce-scatter.38.cloned.1.call-update) | async-done | bytes 589840 | tf_op jit(solution)/shard_map/reduce_scatter | solution.py:447
  (688 shorter events, 302.8 us)
Async XLA Ops:
  7.2 690.4 %reduce-scatter.40.cloned.1.call-start = ((), (), s32[]{:S(2)}) async-start(), calls=%async_computation.17 | async-start | bytes 417792
  10.7 28.4 %copy-start.146 = (f32[768]{0:T(1024)}, f32[768]{0:T(1024)S(1)}, u32[]{:S(2)}) copy-start(f32[768]{0:T(1024)S(1)} %convert_reduce_fusion.22) | copy-start | bytes 9220
  12.0 64.8 %copy-start.90 = (s32[1,1,512]{2,1,0:T(1,128)}, s32[1,1,512]{2,1,0:T(1,128)S(1)}, u32[]{:S(2)}) copy-start(s32[1,1,512]{2,1,0:T(1,128)S(1)} %get-tuple-element.260) | copy-start | bytes 6148
  16.3 74.9 %copy-start.93 = (f32[768]{0:T(1024)}, f32[768]{0:T(1024)S(1)}, u32[]{:S(2)}) copy-start(f32[768]{0:T(1024)S(1)} %get-tuple-element.326) | copy-start | bytes 9220
  39.0 21.8 %copy-start.70 = (bf16[12,64,512]{2,1,0:T(8,128)(2,1)}, bf16[12,64,512]{2,1,0:T(8,128)(2,1)S(1)}, u32[]{:S(2)}) copy-start(bf16[12,64,512]{2,1,0:T(8,128)(2,1)S(1)} %fusion.238) | copy-start | bytes 2359300
  39.1 21.7 %slice-start.18 = ((s8[4718592]{0:T(1024)(128)(4,1)}), s8[4194304]{0:T(1024)(128)(4,1)S(1)}, s32[]{:S(2)}) async-start(s8[4718592]{0:T(1024)(128)(4,1)} %bitcast.849), calls=%async_computation.44 | async-start | bytes 8388608
  40.1 20.8 %copy-start.35 = (f32[512,768]{1,0:T(8,128)}, f32[512,768]{1,0:T(8,128)S(1)}, u32[]{:S(2)}) copy-start(f32[512,768]{1,0:T(8,128)S(1)} %get-tuple-element.270) | copy-start | bytes 4718596
  40.1 20.7 %copy-start.115 = (f32[512]{0:T(512)}, f32[512]{0:T(512)S(1)}, u32[]{:S(2)}) copy-start(f32[512]{0:T(512)S(1)} %broadcast_multiply_fusion.17) | copy-start | bytes 6148
  40.5 95.0 %copy-start.87 = (f32[768]{0:T(1024)}, f32[768]{0:T(1024)S(1)}, u32[]{:S(2)}) copy-start(f32[768]{0:T(1024)S(1)} %get-tuple-element.329) | copy-start | bytes 9220
  66.0 21.9 %collective-permute-start = (bf16[1,512,768]{2,1,0:T(8,128)(2,1)}, bf16[1,512,768]{2,1,0:T(8,128)(2,1)}, u32[]{:S(2)}, u32[]{:S(2)}) collective-permute-start(bf16[1,512,768]{2,1,0:T(8,128)(2,1)} %get-tuple-element.239), channel_id=1, source_target_pairs={{0,16},{1,17},{2,18},{3,19},{4,20},{5,21},{6,22},{7,23},{8,24},{9,... | collective-permute-start | bytes 2359304 | tf_op jit(solution)/shard_map/ppermute | solution.py:20
  113.9 21.6 %copy-start.71 = (bf16[12,64,512]{2,1,0:T(8,128)(2,1)}, bf16[12,64,512]{2,1,0:T(8,128)(2,1)S(1)}, u32[]{:S(2)}) copy-start(bf16[12,64,512]{2,1,0:T(8,128)(2,1)S(1)} %fusion.237) | copy-start | bytes 2359300
  114.0 21.6 %slice-start.20 = ((s8[4718592]{0:T(1024)(128)(4,1)}), s8[4194304]{0:T(1024)(128)(4,1)S(1)}, s32[]{:S(2)}) async-start(s8[4718592]{0:T(1024)(128)(4,1)} %bitcast.851), calls=%async_computation.46 | async-start | bytes 8388608
  141.6 116.5 %copy-start.85 = (f32[4,768]{1,0:T(4,128)}, f32[4,768]{1,0:T(4,128)S(1)}, u32[]{:S(2)}) copy-start(f32[4,768]{1,0:T(4,128)S(1)} %get-tuple-element.290) | copy-start | bytes 36868
  141.6 59.6 %collective-permute-start.1 = (bf16[1,512,768]{2,1,0:T(8,128)(2,1)}, bf16[1,512,768]{2,1,0:T(8,128)(2,1)}, u32[]{:S(2)}, u32[]{:S(2)}) collective-permute-start(bf16[1,512,768]{2,1,0:T(8,128)(2,1)} %get-tuple-element.241), channel_id=1, source_target_pairs={{0,16},{1,17},{2,18},{3,19},{4,20},{5,21},{6,22},{7,23},{8,24},{9,... | collective-permute-start | bytes 2359304 | tf_op jit(solution)/shard_map/ppermute | solution.py:20
  173.7 22.5 %copy-start.134 = (f32[4]{0:T(128)}, f32[4]{0:T(128)S(1)}, u32[]{:S(2)}) copy-start(f32[4]{0:T(128)S(1)} %get-tuple-element.291) | copy-start | bytes 52
  175.1 21.1 %copy-start.136 = (f32[4]{0:T(128)}, f32[4]{0:T(128)S(1)}, u32[]{:S(2)}) copy-start(f32[4]{0:T(128)S(1)} %get-tuple-element.173) | copy-start | bytes 52
  227.4 26.4 %slice-start.22 = ((s8[4718592]{0:T(1024)(128)(4,1)}), s8[4194304]{0:T(1024)(128)(4,1)S(1)}, s32[]{:S(2)}) async-start(s8[4718592]{0:T(1024)(128)(4,1)} %bitcast.853), calls=%async_computation.48 | async-start | bytes 8388608
  228.8 25.0 %slice-start.23 = ((s8[4718592]{0:T(1024)(128)(4,1)}), s8[524288]{0:T(1024)(128)(4,1)S(1)}, s32[]{:S(2)}) async-start(s8[4718592]{0:T(1024)(128)(4,1)} %bitcast.853), calls=%async_computation.49 | async-start | bytes 1048576
  268.4 21.0 %copy-start.4 = (f32[3,512,3072]{2,1,0:T(8,128)}, f32[3,512,3072]{2,1,0:T(8,128)S(1)}, u32[]{:S(2)}) copy-start(f32[3,512,3072]{2,1,0:T(8,128)S(1)} %pad_maximum_fusion) | copy-start | bytes 56623108
  352.0 77.8 %copy-start.82 = (f32[4,768]{1,0:T(4,128)}, f32[4,768]{1,0:T(4,128)S(1)}, u32[]{:S(2)}) copy-start(f32[4,768]{1,0:T(4,128)S(1)} %get-tuple-element.286) | copy-start | bytes 36868
  375.8 24.9 %copy-start.138 = (f32[4]{0:T(128)}, f32[4]{0:T(128)S(1)}, u32[]{:S(2)}) copy-start(f32[4]{0:T(128)S(1)} %get-tuple-element.287) | copy-start | bytes 52
  375.8 24.6 %copy-start.77 = (bf16[64,768]{1,0:T(8,128)(2,1)S(1)}, bf16[64,768]{1,0:T(8,128)(2,1)}, u32[]{:S(2)}) copy-start(bf16[64,768]{1,0:T(8,128)(2,1)} %reshape.1415) | copy-start | bytes 294916
  381.0 48.9 %collective-permute-start.4 = (bf16[1,512,768]{2,1,0:T(8,128)(2,1)}, bf16[1,512,768]{2,1,0:T(8,128)(2,1)}, u32[]{:S(2)}, u32[]{:S(2)}) collective-permute-start(bf16[1,512,768]{2,1,0:T(8,128)(2,1)} %fusion.240), channel_id=1, source_target_pairs={{16,0},{17,1},{18,2},{19,3},{20,4},{21,5},{22,6},{23,7},{24,8},{25... | collective-permute-start | bytes 2359304 | tf_op jit(solution)/shard_map/ppermute | solution.py:20
  429.9 25.4 %slice-start.12 = ((s8[4718592]{0:T(1024)(128)(4,1)}), s8[4194304]{0:T(1024)(128)(4,1)S(1)}, s32[]{:S(2)}) async-start(s8[4718592]{0:T(1024)(128)(4,1)} %bitcast.738), calls=%async_computation.38 | async-start | bytes 8388608
  429.9 25.4 %slice-start.30 = ((s8[4718592]{0:T(1024)(128)(4,1)}), s8[4194304]{0:T(1024)(128)(4,1)S(1)}, s32[]{:S(2)}) async-start(s8[4718592]{0:T(1024)(128)(4,1)} %bitcast.861), calls=%async_computation.56 | async-start | bytes 8388608
  473.9 23.4 %copy-start.176 = (bf16[12,64,512]{2,1,0:T(8,128)(2,1)}, bf16[12,64,512]{2,1,0:T(8,128)(2,1)S(1)}, u32[]{:S(2)}) copy-start(bf16[12,64,512]{2,1,0:T(8,128)(2,1)S(1)} %get-tuple-element.317) | copy-start | bytes 2359300
  497.8 25.0 %slice-start.10 = ((s8[4718592]{0:T(1024)(128)(4,1)}), s8[524288]{0:T(1024)(128)(4,1)S(1)}, s32[]{:S(2)}) async-start(s8[4718592]{0:T(1024)(128)(4,1)} %bitcast.736), calls=%async_computation.36 | async-start | bytes 1048576
  500.0 22.8 %collective-permute-start.5 = (bf16[1,512,768]{2,1,0:T(8,128)(2,1)S(1)}, bf16[1,512,768]{2,1,0:T(8,128)(2,1)S(1)}, u32[]{:S(2)}, u32[]{:S(2)}) collective-permute-start(bf16[1,512,768]{2,1,0:T(8,128)(2,1)S(1)} %convert_bitcast_fusion), channel_id=1, source_target_pairs={{16,0},{17,1},{18,2},{19,3},{20,4},{21,5},{22,6},{23,7},{24,8},{25... | collective-permute-start | bytes 2359304 | tf_op jit(solution)/shard_map/ppermute | solution.py:20
  501.3 21.5 %slice-start.11 = ((s8[4718592]{0:T(1024)(128)(4,1)}), s8[4194304]{0:T(1024)(128)(4,1)S(1)}, s32[]{:S(2)}) async-start(s8[4718592]{0:T(1024)(128)(4,1)} %bitcast.736), calls=%async_computation.37 | async-start | bytes 8388608
  501.3 21.5 %copy-start.34 = (f32[512,768]{1,0:T(8,128)S(1)}, f32[512,768]{1,0:T(8,128)}, u32[]{:S(2)}) copy-start(f32[512,768]{1,0:T(8,128)} %get-tuple-element.301) | copy-start | bytes 4718596
  501.3 23.7 %slice-start.26 = ((s8[4718592]{0:T(1024)(128)(4,1)}), s8[4194304]{0:T(1024)(128)(4,1)S(1)}, s32[]{:S(2)}) async-start(s8[4718592]{0:T(1024)(128)(4,1)} %bitcast.857), calls=%async_computation.52 | async-start | bytes 8388608
  522.8 22.6 %slice-start.14 = ((s8[4718592]{0:T(1024)(128)(4,1)}), s8[4194304]{0:T(1024)(128)(4,1)S(1)}, s32[]{:S(2)}) async-start(s8[4718592]{0:T(1024)(128)(4,1)} %bitcast.740), calls=%async_computation.40 | async-start | bytes 8388608
  522.8 22.6 %slice-start.32 = ((s8[4718592]{0:T(1024)(128)(4,1)}), s8[4194304]{0:T(1024)(128)(4,1)S(1)}, s32[]{:S(2)}) async-start(s8[4718592]{0:T(1024)(128)(4,1)} %bitcast.863), calls=%async_computation.58 | async-start | bytes 8388608
  588.7 111.7 %reduce-scatter.42.cloned.1.call-start = ((), (), s32[]{:S(2)}) async-start(), calls=%async_computation.18 | async-start | bytes 417792
  590.6 168.0 %reduce-scatter.44.cloned.1.call-start = ((), (), s32[]{:S(2)}) async-start(), calls=%async_computation.19 | async-start | bytes 417792
  592.3 224.7 %reduce-scatter.46.cloned.1.call-start = ((), (), s32[]{:S(2)}) async-start(), calls=%async_computation.20 | async-start | bytes 417792
  594.0 281.0 %reduce-scatter.48.cloned.1.call-start = ((), (), s32[]{:S(2)}) async-start(), calls=%async_computation.21 | async-start | bytes 417792
  595.7 337.7 %reduce-scatter.52.cloned.1.call-start = ((), (), s32[]{:S(2)}) async-start(), calls=%async_computation.23 | async-start | bytes 417792
  597.4 394.1 %reduce-scatter.54.cloned.1.call-start = ((), (), s32[]{:S(2)}) async-start(), calls=%async_computation.24 | async-start | bytes 417792
  599.1 450.9 %reduce-scatter.56.cloned.1.call-start = ((), (), s32[]{:S(2)}) async-start(), calls=%async_computation.25 | async-start | bytes 417792
  600.8 511.5 %reduce-scatter.50.cloned.1.call-start = ((), (), s32[]{:S(2)}) async-start(), calls=%async_computation.22 | async-start | bytes 1671168
  603.3 575.6 %reduce-scatter.34.cloned.1.call-start = ((), (), s32[]{:S(2)}) async-start(), calls=%async_computation.14 | async-start | bytes 2506752 | tf_op jit(solution)/shard_map/reduce_scatter | solution.py:447
  608.7 663.9 %reduce-scatter.32.cloned.1.call-start = ((), (), s32[]{:S(2)}) async-start(), calls=%async_computation.13 | async-start | bytes 7520256 | tf_op jit(solution)/shard_map/reduce_scatter | solution.py:447
  626.2 762.4 %reduce-scatter.36.cloned.1.call-start = ((), (), s32[]{:S(2)}) async-start(), calls=%async_computation.15 | async-start | bytes 10027008 | tf_op jit(solution)/shard_map/reduce_scatter | solution.py:447
  644.0 860.4 %reduce-scatter.38.cloned.1.call-start = ((), (), s32[]{:S(2)}) async-start(), calls=%async_computation.16 | async-start | bytes 10027008 | tf_op jit(solution)/shard_map/reduce_scatter | solution.py:447
  676.8 437.0 %collective-permute-start.6 = (bf16[2,1,512,384]{3,2,1,0:T(8,128)(2,1)}, bf16[2,1,512,384]{3,2,1,0:T(8,128)(2,1)}, u32[]{:S(2)}, u32[]{:S(2)}) collective-permute-start(bf16[2,1,512,384]{3,2,1,0:T(8,128)(2,1)} %fusion.168), channel_id=1, source_target_pairs={{0,16},{16,0},{1,17},{17,1},{2,18},{18,2},{3,19},{19,3},{4,20},{20... | collective-permute-start | bytes 2359304 | tf_op jit(solution)/shard_map/ppermute | solution.py:26
  676.8 20.3 %collective-permute-start.2 = (bf16[2,4,384]{2,1,0:T(4,128)(2,1)S(1)}, bf16[2,4,384]{2,1,0:T(4,128)(2,1)S(1)}, u32[]{:S(2)}, u32[]{:S(2)}) collective-permute-start(bf16[2,4,384]{2,1,0:T(4,128)(2,1)S(1)} %fusion.333), channel_id=1, source_target_pairs={{0,16},{16,0},{1,17},{17,1},{2,18},{18,2},{3,19},{19,3},{4,20},{20... | collective-permute-start | bytes 18440 | tf_op jit(solution)/shard_map/ppermute | solution.py:26
  678.9 17.6 %collective-permute-start.3 = (bf16[2,4]{1,0:T(2,128)(2,1)S(1)}, bf16[2,4]{1,0:T(2,128)(2,1)S(1)}, u32[]{:S(2)}, u32[]{:S(2)}) collective-permute-start(bf16[2,4]{1,0:T(2,128)(2,1)S(1)} %fusion.352), channel_id=1, source_target_pairs={{0,16},{16,0},{1,17},{17,1},{2,18},{18,2},{3,19},{19,3},{4,20},{20... | collective-permute-start | bytes 56 | tf_op jit(solution)/shard_map/ppermute | solution.py:26
  (185 other events, 1251.9 us)
Sparse Core Ops, SparseCore 0:
  588.8 53.0 reduce-scatter.39
  645.8 54.5 reduce-scatter.41
  703.9 54.5 reduce-scatter.43
  762.3 54.6 reduce-scatter.45
  820.3 54.5 reduce-scatter.47
  878.7 54.6 reduce-scatter.51
  936.9 54.5 reduce-scatter.53
  995.4 54.6 reduce-scatter.55
  1053.7 58.5 reduce-scatter.49
  1116.9 61.9 reduce-scatter.33
  1183.5 89.0 reduce-scatter.31
  1277.7 110.8 reduce-scatter.35
  1393.3 111.0 reduce-scatter.37
where the time goes:
time: 1520 us; the launch traced here: 1510 us
  waiting for transfers between devices  824 us (54%)
  matrix products  347 us (23%)
  local copies, waits for them, and re-layouts  116 us (8%)
  other arithmetic  112 us (7%)
  blocking collectives  78.5 us (5%)
  between operations  17.1 us (1%)
  starting transfers between devices  16.5 us (1%)
    unnamed x22, waiting for transfers between devices  404 us
    reduce_scatter x4, waiting for transfers between devices, local(): lax.psum_scatter(tuple((grad_part[None] for grad_part in totals)), 'dp',...  388 us
    dot_general x3, matrix products, layer_back_input(): jnp.dot(d_branch_two, w_out.T, preferred_element_type=jnp.float32)  60.2 us
    dot_general x14, matrix products, contract_rows(): lax.dot_general(left, right, (((0,), (0,)), ((), ())), preferred_element_...  59.8 us
    dot_general x3, matrix products, layer_forward(): jnp.dot(hidden_low, w_in, preferred_element_type=jnp.float32) + b_in  59.8 us
    unnamed x444, local copies, waits for them, and re-layouts  47.2 us
    all_gather x2, blocking collectives, contrast_head(): lax.all_gather(unit_low, 'dp', axis=0, tiled=True)  43.7 us
    all_gather x2, blocking collectives, contrast_head(): all_scores = lax.all_gather(d_logits, 'dp', axis=0, tiled=True)  34.9 us
  transfers between devices with their start and end apart: 20, of which 15 were waited for; matrix products, arithmetic and copies ran while one was open for 11% of the time, Pallas kernels for 0%

commit v1 on v0

v1 whole, which is shorter than its diff:
```python
import functools
import jax, jax.numpy as jnp
from jax import lax
from jax.experimental import pallas as pl
from jax.experimental.pallas import tpu as pltpu
from jax.sharding import PartitionSpec as P

HEADS = 12
HEAD_DIM = 64
SEGS = 4
UNIT_EPS = 1e-06
TEMPER = 20.0
MASK_FILL = 1000000000.0
NORM_EPS = 1e-12
BF = jnp.bfloat16
F32 = jnp.float32
VMEM_LIMIT = 60 * 2**20
MESH = pl.DeviceIdType.MESH
ANY = pl.BlockSpec(memory_space=pl.ANY)
VM = pl.BlockSpec(memory_space=pltpu.VMEM)


def dot(a, b):
    return jnp.dot(a, b, preferred_element_type=F32)


def dot_nt(a, b):
    return lax.dot_general(a, b, (((1,), (1,)), ((), ())), preferred_element_type=F32)


def dot_tn(a, b):
    return lax.dot_general(a, b, (((0,), (0,)), ((), ())), preferred_element_type=F32)


def split3(v):
    hi = v.astype(BF)
    rest = v - hi.astype(F32)
    mid = rest.astype(BF)
    low = (rest - mid.astype(F32)).astype(BF)
    return hi, mid, low


def members(seg_row):
    rows = lax.broadcasted_iota(jnp.int32, (16, seg_row.shape[1]), 0)
    return jnp.where(rows == seg_row, 1.0, 0.0).astype(BF)


def normed_rows(rows):
    centre = rows - jnp.mean(rows, axis=-1, keepdims=True)
    scale = lax.rsqrt(jnp.mean(centre * centre, axis=-1, keepdims=True) + NORM_EPS)
    return centre * scale, scale


def gelu_pair(u):
    mag = jnp.abs(u)
    t = 1.0 / (1.0 + (0.3275911 * 0.7071067811865476) * mag)
    e = jnp.exp(-0.5 * (u * u))
    poly = t * (0.127414796 + t * (-0.142248368 + t * (0.7107068705 + t * (-0.7265760135 + t * 0.5307027145))))
    tail = poly * e
    cdf = jnp.where(u >= 0.0, 1.0 - tail, tail)
    return u * cdf, cdf + (u * 0.3989422804014327) * e


def fwd_kernel(tb, fc, qb,
    x_h, seg, wqkv_h, bq, bv, wat_h, bat, g1, b1, win_h, bin_, wout_h, bout, g2, b2,
    pool_o, x_o, qkv_h, lse_o, c_h, z1_h, s1_o, hb_h, gp_h, act_h, z2_h, s2_o,
    x_s, wqkv, wat, win, wout, qkv, bias, c_s, h_s, hb_s, z1_s, gp_s, act_s, z2_s, y_s, lse_s, yf,
    insem, wsem, outsem, send_sem, recv_sem):
    sec = lax.axis_index("section")
    other = {"section": 1 - sec}
    M, T, D = x_s.shape
    FF = win.shape[1]
    nb = T // tb

    ws = [pltpu.make_async_copy(a, b, wsem.at[i]) for i, (a, b) in enumerate(
        ((wqkv_h, wqkv), (wat_h, wat), (win_h, win), (wout_h, wout)))]
    ws[0].start()
    barrier = pltpu.get_barrier_semaphore()
    pl.semaphore_signal(barrier, inc=1, device_id=other, device_id_type=MESH)

    @pl.when(sec == 0)
    def _():
        for m in range(M):
            pltpu.make_async_copy(x_h.at[m], x_s.at[m], insem.at[m]).start()
    for w in ws[1:]:
        w.start()
    pl.semaphore_wait(barrier, 1)

    lane = lax.broadcasted_iota(jnp.int32, (1, 128), 1)
    low_half = lane < HEAD_DIM

    def out_copies(m):
        pairs = [(x_s, x_o), (qkv, qkv_h), (c_s, c_h), (hb_s, hb_h), (z1_s, z1_h), (act_s, act_h), (gp_s, gp_h), (z2_s, z2_h)]
        return [pltpu.make_async_copy(a.at[m], b.at[m], outsem.at[m, i]) for i, (a, b) in enumerate(pairs)]

    def handoff(m, i):
        r = pl.ds(i * tb if isinstance(i, int) else pl.multiple_of(i * tb, tb), tb)
        return pltpu.make_async_remote_copy(src_ref=y_s.at[m, r], dst_ref=x_s.at[m, r], send_sem=send_sem.at[m, i],
            recv_sem=recv_sem.at[m, i], device_id=other, device_id_type=MESH)

    def micro_step(m, _):
        outs = out_copies(m)
        mem = members(seg[pl.ds(m, 1), :])
        bias[...] = (dot_tn(mem, mem) - 1.0) * MASK_FILL

        @pl.when(sec == 0)
        def _():
            pltpu.make_async_copy(x_h.at[m], x_s.at[m], insem.at[m]).wait()

        @pl.when(sec != 0)
        def _():
            for i in range(nb):
                handoff(m, i).wait_recv()
        outs[0].start()

        @pl.when(m == 0)
        def _():
            ws[0].wait()

        def qkv_step(i, _):
            r = pl.ds(pl.multiple_of(i * tb, tb), tb)
            xi = x_s[m, r, :]
            for j, b in ((0, bq), (1, None), (2, bv)):
                cols = slice(j * D, (j + 1) * D)
                v = dot(xi, wqkv[:, cols])
                if b is not None:
                    v = v + b[...].astype(F32)
                qkv[m, r, cols] = v.astype(BF)
            return 0
        lax.fori_loop(0, nb, qkv_step, 0)
        outs[1].start()
        lse_s[...] = jnp.zeros_like(lse_s)

        def att_step(p, _):
            cols = pl.ds(pl.multiple_of(p * 128, 128), 128)
            kcols = pl.ds(pl.multiple_of(p * 128 + D, 128), 128)
            vcols = pl.ds(pl.multiple_of(p * 128 + 2 * D, 128), 128)
            k2 = qkv[m, :, kcols]
            v2 = jnp.concatenate([qkv[m, :, vcols], jnp.ones((T, 128), BF)], axis=1)
            for i in range(T // qb):
                rows = slice(i * qb, (i + 1) * qb)
                q2 = qkv[m, rows, cols] * (HEAD_DIM ** -0.5)
                halves = []
                for h in range(2):
                    pick = low_half if h == 0 else jnp.logical_not(low_half)
                    s = dot_nt(jnp.where(pick, q2, 0), k2) + bias[rows, :]
                    mx = jnp.max(s, axis=-1, keepdims=True)
                    e = jnp.exp(s - mx).astype(BF)
                    c = dot(e, v2)
                    l = c[:, 128:]
                    halves.append(c[:, :128] / l)
                    lse_s[rows, :] = jnp.where(lane == 2 * p + h, mx + jnp.log(l), lse_s[rows, :])
                c_s[m, rows, cols] = jnp.where(low_half, halves[0], halves[1]).astype(BF)
            return 0
        lax.fori_loop(0, HEADS // 2, att_step, 0)
        outs[2].start()
        lse_o[m] = jnp.transpose(lse_s[...])[:16, :]

        @pl.when(m == 0)
        def _():
            ws[1].wait()

        def proj_step(i, _):
            r = pl.ds(pl.multiple_of(i * tb, tb), tb)
            r1 = x_s[m, r, :].astype(F32) + dot(c_s[m, r, :], wat[...]) + bat[...].astype(F32)
            z, scale = normed_rows(r1)
            h = z * g1[...].astype(F32) + b1[...].astype(F32)
            h_s[r, :] = h
            hb_s[m, r, :] = h.astype(BF)
            z1_s[m, r, :] = z.astype(BF)
            s1_o[m, r, :] = scale
            return 0
        lax.fori_loop(0, nb, proj_step, 0)
        outs[3].start()
        outs[4].start()

        @pl.when(m == 0)
        def _():
            ws[2].wait()
            ws[3].wait()

        def ffn_step(i, _):
            r = pl.ds(pl.multiple_of(i * tb, tb), tb)
            hi = hb_s[m, r, :]
            acc = h_s[r, :] + bout[...].astype(F32)
            nj = FF // fc
            us = [dot(hi, win[:, :fc])]
            for j in range(nj):
                cols = slice(j * fc, (j + 1) * fc)
                if j + 1 < nj:
                    us.append(dot(hi, win[:, (j + 1) * fc:(j + 2) * fc]))
                f, gp = gelu_pair(us[j] + bin_[:, cols].astype(F32))
                f = f.astype(BF)
                act_s[m, r, cols] = f
                gp_s[m, r, cols] = gp.astype(BF)
                acc = acc + dot(f, wout[cols, :])
            z, scale = normed_rows(acc)
            y = z * g2[...].astype(F32) + b2[...].astype(F32)
            z2_s[m, r, :] = z.astype(BF)
            s2_o[m, r, :] = scale
            y_s[m, r, :] = y.astype(BF)
            yf[r, :] = y

            @pl.when(sec == 0)
            def _():
                handoff(m, i).start()
            return 0
        lax.fori_loop(0, nb, ffn_step, 0)
        for o in outs[5:]:
            o.start()
        hi, mid, low = split3(yf[...])
        pool_o[m] = (dot(mem, hi) + dot(mem, mid)) + dot(mem, low)
        return 0
    lax.fori_loop(0, M, micro_step, 0)
    for m in range(M):
        for o in out_copies(m):
            o.wait()

    @pl.when(sec == 0)
    def _():
        for m in range(M):
            for i in range(nb):
                handoff(m, i).wait_send()


def stack_fwd(x, seg, weights, tb=256, fc=768, qb=256):
    M, T, D = x.shape
    FF = weights[7].shape[1]
    sds = jax.ShapeDtypeStruct
    out_shape = (sds((M, 16, D), F32), sds((M, T, D), BF), sds((M, T, 3 * D), BF), sds((M, 16, T), F32), sds((M, T, D), BF),
        sds((M, T, D), BF), sds((M, T, 1), F32), sds((M, T, D), BF), sds((M, T, FF), BF), sds((M, T, FF), BF), sds((M, T, D), BF), sds((M, T, 1), F32))
    out_specs = (VM, ANY, ANY, VM, ANY, ANY, VM, ANY, ANY, ANY, ANY, VM)
    V = pltpu.VMEM
    S = pltpu.SemaphoreType.DMA
    nb = T // tb
    scratch = [V((M, T, D), BF), V((D, 3 * D), BF), V((D, D), BF), V((D, FF), BF), V((FF, D), BF), V((M, T, 3 * D), BF), V((T, T), F32),
        V((M, T, D), BF), V((T, D), F32), V((M, T, D), BF), V((M, T, D), BF), V((M, T, FF), BF), V((M, T, FF), BF), V((M, T, D), BF), V((M, T, D), BF),
        V((T, 128), F32), V((T, D), F32), S((M,)), S((4,)), S((M, 8)), S((M, nb)), S((M, nb))]
    in_specs = (ANY, VM, ANY, VM, VM, ANY, VM, VM, VM, ANY, VM, ANY, VM, VM, VM)
    return pl.pallas_call(functools.partial(fwd_kernel, tb, fc, qb), out_shape=out_shape, in_specs=in_specs, out_specs=out_specs,
        scratch_shapes=scratch, compiler_params=pltpu.CompilerParams(vmem_limit_bytes=VMEM_LIMIT, collective_id=0, has_side_effects=True),
        name="stack_fwd")(x, seg, *weights)


def rowsum8(v):
    return jnp.sum(v.reshape(v.shape[0] // 8, 8, v.shape[1]), axis=0)


def bwd_kernel(tb, fc, kb,
    seg, dp, lse, s1, s2, qkv_h, c_h, z1_h, gp_h, z2_h, wqkv_h, wat_h, g1, win_h, wout_h, g2,
    vec_o, dx_h, db2_h, du_h, db1_h, dqkv_h,
    dyr, wqkv, wat, win, wout, qkv, c_s, z1, gp, z2, bias, dy_s, dr1, dc, delta, du, db2, db1, dqkv, dx, dxb, vacc, bacc,
    insem, wsem, outsem, send_sem, recv_sem):
    sec = lax.axis_index("section")
    other = {"section": 1 - sec}
    M, T, D = c_s.shape
    FF = win.shape[1]
    nb = T // tb

    ws = [pltpu.make_async_copy(a, b, wsem.at[i]) for i, (a, b) in enumerate(
        ((wout_h, wout), (win_h, win), (wat_h, wat), (wqkv_h, wqkv)))]

    def in_copies(m):
        pairs = [(z2_h, z2), (gp_h, gp), (z1_h, z1), (c_h, c_s), (qkv_h, qkv)]
        return [pltpu.make_async_copy(a.at[m], b.at[m], insem.at[m, i]) for i, (a, b) in enumerate(pairs)]
    first = in_copies(0)
    first[0].start()
    ws[0].start()
    barrier = pltpu.get_barrier_semaphore()
    pl.semaphore_signal(barrier, inc=1, device_id=other, device_id_type=MESH)
    for a, b in zip(first[1:], ws[1:]):
        a.start()
        b.start()
    first[4].start()
    for m in range(1, M):
        for a in in_copies(m):
            a.start()
    vacc[...] = jnp.zeros_like(vacc)
    bacc[...] = jnp.zeros_like(bacc)
    pl.semaphore_wait(barrier, 1)

    lane = lax.broadcasted_iota(jnp.int32, (1, 128), 1)
    low_half = lane < HEAD_DIM
    indicator = jnp.where(lax.broadcasted_iota(jnp.int32, (16, D), 1) // HEAD_DIM == lax.broadcasted_iota(jnp.int32, (16, D), 0), 1.0, 0.0).astype(BF)

    def out_copies(m):
        pairs = [(db2, db2_h), (du, du_h), (db1, db1_h), (dqkv, dqkv_h), (dx, dx_h)]
        return [pltpu.make_async_copy(a.at[m], b.at[m], outsem.at[m, i]) for i, (a, b) in enumerate(pairs)]

    def handoff(m, i):
        r = pl.ds(i * tb if isinstance(i, int) else pl.multiple_of(i * tb, tb), tb)
        return pltpu.make_async_remote_copy(src_ref=dxb.at[m, r], dst_ref=dyr.at[m, r], send_sem=send_sem.at[m, i],
            recv_sem=recv_sem.at[m, i], device_id=other, device_id_type=MESH)

    def norm_pull(z, scale, gain, dy):
        g = dy * gain
        return scale * (g - jnp.mean(g, axis=-1, keepdims=True) - z * jnp.mean(g * z, axis=-1, keepdims=True))

    def micro_step(m, _):
        ins = in_copies(m)
        outs = out_copies(m)
        mem = members(seg[pl.ds(m, 1), :])
        bias[...] = (dot_tn(mem, mem) - 1.0) * MASK_FILL
        dp3 = jnp.concatenate(split3(dp[m]), axis=0)

        @pl.when(sec == 0)
        def _():
            for i in range(nb):
                handoff(m, i).wait_recv()

        @pl.when(m == 0)
        def _():
            ws[0].wait()
            ws[1].wait()
            ws[2].wait()
        for a in ins[:4]:
            a.wait()

        def tok_step(i, _):
            r = pl.ds(pl.multiple_of(i * tb, tb), tb)

            @pl.when(sec == 0)
            def _():
                dy_s[...] = dyr[m, r, :].astype(F32)

            @pl.when(sec != 0)
            def _():
                blk = members(seg[pl.ds(m, 1), r])
                dy_s[...] = dot_tn(jnp.concatenate([blk, blk, blk], axis=0), dp3)
            dy = dy_s[...]
            z = z2[m, r, :].astype(F32)
            dr2 = norm_pull(z, s2[m, r, :], g2[...].astype(F32), dy)
            vacc[0] += rowsum8(dy * z)
            vacc[1] += rowsum8(dy)
            d2 = dr2.astype(BF)
            db2[m, r, :] = d2
            vacc[2] += rowsum8(d2.astype(F32))
            dh = dr2
            nj = FF // fc
            dfs = [dot_nt(d2, wout[:fc, :])]
            for j in range(nj):
                cols = slice(j * fc, (j + 1) * fc)
                if j + 1 < nj:
                    dfs.append(dot_nt(d2, wout[(j + 1) * fc:(j + 2) * fc, :]))
                dub = (dfs[j] * gp[m, r, cols].astype(F32)).astype(BF)
                du[m, r, cols] = dub
                bacc[:, cols] += rowsum8(dub.astype(F32))
                dh = dh + dot_nt(dub, win[:, cols])
            z = z1[m, r, :].astype(F32)
            d1 = norm_pull(z, s1[m, r, :], g1[...].astype(F32), dh)
            vacc[3] += rowsum8(dh * z)
            vacc[4] += rowsum8(dh)
            dr1[r, :] = d1
            d1 = d1.astype(BF)
            db1[m, r, :] = d1
            vacc[5] += rowsum8(d1.astype(F32))
            dcb = dot_nt(d1, wat[...]).astype(BF)
            dc[r, :] = dcb
            prod = dcb.astype(F32) * c_s[m, r, :].astype(F32)
            hi = prod.astype(BF)
            low = (prod - hi.astype(F32)).astype(BF)
            delta[:, r] = dot_nt(indicator, hi) + dot_nt(indicator, low)
            return 0
        lax.fori_loop(0, nb, tok_step, 0)
        for o in outs[:3]:
            o.start()
        ins[4].wait()

        def att_step(p, _):
            cols = pl.ds(pl.multiple_of(p * 128, 128), 128)
            kcols = pl.ds(pl.multiple_of(p * 128 + D, 128), 128)
            vcols = pl.ds(pl.multiple_of(p * 128 + 2 * D, 128), 128)
            q2 = qkv[m, :, cols] * (HEAD_DIM ** -0.5)
            dc2 = dc[:, cols]
            dqt = jnp.zeros((128, T), F32)
            for i in range(T // kb):
                rows = slice(i * kb, (i + 1) * kb)
                k2 = qkv[m, rows, kcols]
                v2 = qkv[m, rows, vcols]
                dks, dvs = [], []
                for h in range(2):
                    pick = low_half if h == 0 else jnp.logical_not(low_half)
                    kh = jnp.where(pick, k2, 0)
                    vh = jnp.where(pick, v2, 0)
                    st = dot_nt(kh, q2) + bias[rows, :]
                    pt = jnp.exp(st - lse[m, pl.ds(2 * p + h, 1), :])
                    dpt = dot_nt(vh, dc2)
                    da = (pt * (dpt - delta[pl.ds(2 * p + h, 1), :])).astype(BF)
                    dvs.append(dot(pt.astype(BF), dc2))
                    dks.append(dot(da, q2))
                    dqt = dqt + dot_tn(kh, da)
                dqkv[m, rows, kcols] = jnp.where(low_half, dks[0], dks[1]).astype(BF)
                dqkv[m, rows, vcols] = jnp.where(low_half, dvs[0], dvs[1]).astype(BF)
            dqkv[m, :, cols] = (jnp.transpose(dqt) * (HEAD_DIM ** -0.5)).astype(BF)
            return 0
        lax.fori_loop(0, HEADS // 2, att_step, 0)
        outs[3].start()

        @pl.when(m == 0)
        def _():
            ws[3].wait()

        def dx_step(i, _):
            r = pl.ds(pl.multiple_of(i * tb, tb), tb)
            v = dr1[r, :] + dot_nt(dqkv[m, r, :], wqkv[...])
            dx[m, r, :] = v
            dxb[m, r, :] = v.astype(BF)
            vacc[6] += rowsum8(dqkv[m, r, :D].astype(F32))
            vacc[7] += rowsum8(dqkv[m, r, 2 * D:].astype(F32))

            @pl.when(sec != 0)
            def _():
                handoff(m, i).start()
            return 0
        lax.fori_loop(0, nb, dx_step, 0)
        outs[4].start()
        return 0
    lax.fori_loop(0, M, micro_step, 0)
    vec_o[...] = jnp.concatenate([jnp.sum(vacc[...], axis=1)]
        + [jnp.sum(bacc[:, j * D:(j + 1) * D], axis=0, keepdims=True) for j in range(FF // D)] + [jnp.zeros((4, D), F32)], axis=0)
    for m in range(M):
        for o in out_copies(m):
            o.wait()

    @pl.when(sec != 0)
    def _():
        for m in range(M):
            for i in range(nb):
                handoff(m, i).wait_send()


def stack_bwd(seg, dp, stash, weights, tb=256, fc=768, kb=256):
    qkv, lse, c, z1, s1, gp, z2, s2 = stash
    wqkv, bq, bv, wat, bat, g1, b1, win, bin_, wout, bout, g2, b2 = weights
    M, T, D = c.shape
    FF = win.shape[1]
    sds = jax.ShapeDtypeStruct
    out_shape = (sds((16, D), F32), sds((M, T, D), F32), sds((M, T, D), BF), sds((M, T, FF), BF), sds((M, T, D), BF), sds((M, T, 3 * D), BF))
    out_specs = (VM, ANY, ANY, ANY, ANY, ANY)
    V = pltpu.VMEM
    S = pltpu.SemaphoreType.DMA
    nb = T // tb
    scratch = [V((M, T, D), BF), V((D, 3 * D), BF), V((D, D), BF), V((D, FF), BF), V((FF, D), BF),
        V((M, T, 3 * D), BF), V((M, T, D), BF), V((M, T, D), BF), V((M, T, FF), BF), V((M, T, D), BF),
        V((T, T), F32), V((tb, D), F32), V((T, D), F32), V((T, D), BF), V((16, T), F32),
        V((M, T, FF), BF), V((M, T, D), BF), V((M, T, D), BF), V((M, T, 3 * D), BF), V((M, T, D), F32), V((M, T, D), BF),
        V((8, 8, D), F32), V((8, FF), F32), S((M, 5)), S((4,)), S((M, 5)), S((M, nb)), S((M, nb))]
    in_specs = (VM, VM, VM, VM, VM, ANY, ANY, ANY, ANY, ANY, ANY, ANY, VM, ANY, ANY, VM)
    return pl.pallas_call(functools.partial(bwd_kernel, tb, fc, kb), out_shape=out_shape, in_specs=in_specs, out_specs=out_specs,
        scratch_shapes=scratch, compiler_params=pltpu.CompilerParams(vmem_limit_bytes=VMEM_LIMIT, collective_id=1, has_side_effects=True),
        name="stack_bwd")(seg, dp, lse, s1, s2, qkv, c, z1, gp, z2, wqkv, wat, g1, win, wout, g2)


def contrast_head(pool, seg, pairs, all_pairs):
    M, S = pairs.shape
    D = pool.shape[-1]
    counts = jnp.sum((seg[:, :, None] == jnp.arange(SEGS)).astype(F32), axis=1)[:, :, None]
    pooled = pool[:, :SEGS] / counts
    radius = lax.rsqrt(jnp.sum(pooled * pooled, axis=-1, keepdims=True) + UNIT_EPS)
    unit = (pooled * radius).astype(BF)
    every = lax.all_gather(unit, "dp", axis=1, tiled=True)
    total = every.shape[1]
    start = lax.axis_index("dp") * S
    logits = TEMPER * jnp.einsum("mgd,mkd->mgk", every, every, preferred_element_type=F32)
    cols = jnp.arange(total)
    logits = jnp.where(cols[:, None] == cols[None, :], -MASK_FILL, logits)
    peak = jnp.max(logits, axis=-1, keepdims=True)
    exponent = jnp.exp(logits - peak)
    denom = jnp.sum(exponent, axis=-1, keepdims=True)
    target = cols[None, None, :] == all_pairs[:, :, None]
    loss = peak[..., 0] + jnp.log(denom[..., 0]) - jnp.sum(jnp.where(target, logits, 0.0), axis=-1)
    dl = (exponent / denom - target.astype(F32)).astype(BF)
    rows = lax.dynamic_slice_in_dim(dl, start, S, 1)
    columns = lax.dynamic_slice_in_dim(dl, start, S, 2)
    dn = TEMPER * (jnp.einsum("mgk,mkd->mgd", rows, every, preferred_element_type=F32)
        + jnp.einsum("mkg,mkd->mgd", columns, every, preferred_element_type=F32))
    dp = radius * dn - radius * radius * radius * jnp.sum(pooled * dn, axis=-1, keepdims=True) * pooled
    loss = lax.dynamic_slice_in_dim(loss, start, S, 1)
    return pooled, loss, jnp.pad(dp / counts, ((0, 0), (0, 16 - SEGS), (0, 0)))


def scattered(grads):
    count = lax.axis_size("dp")
    packed = jnp.concatenate([g.reshape(count, -1) for g in grads], axis=1)
    part = lax.psum_scatter(packed, "dp", scatter_dimension=0, tiled=True)[0].astype(F32)
    outs, at = [], 0
    for g in grads:
        size = g.size // count
        outs.append(part[at:at + size].reshape((1, g.shape[0] // count) + g.shape[1:]))
        at += size
    return outs


def swapped(value):
    return lax.ppermute(value, "section", [(0, 1), (1, 0)])


def local(hidden_in, seg_ids, pair_ids, w_qkv, b_query, b_value, w_attn_out, b_attn_out, ln1_gain, ln1_bias, w_in, b_in, w_out, b_out, ln2_gain, ln2_bias):
    M, _, T, D = hidden_in.shape
    sec = lax.axis_index("section")
    first = sec == 0
    seg = seg_ids[:, 0]
    weights = (w_qkv[0], b_query, b_value, w_attn_out[0], b_attn_out, ln1_gain, ln1_bias, w_in[0], b_in, w_out[0], b_out, ln2_gain, ln2_bias)
    all_pairs = lax.all_gather(pair_ids, "dp", axis=1, tiled=True)
    pool, x, qkv, lse, c, z1, s1, hb, gp, act, z2, s2 = stack_fwd(hidden_in[:, 0], seg, weights)
    pooled, loss, dp = contrast_head(pool, seg, pair_ids, all_pairs)
    vec, dx, db2, du, db1, dqkv = stack_bwd(seg, dp, (qkv, lse, c, z1, s1, gp, z2, s2), weights)
    big = [jnp.einsum("mta,mtb->ab", a, b, preferred_element_type=F32).astype(BF) for a, b in ((x, dqkv), (c, db1), (hb, du), (act, db2))]
    g_qkv, g_at, g_in, g_out = scattered(big)
    small = scattered([vec[i] for i in range(8)] + [vec[8:8 + w_in.shape[2] // D].reshape(-1)])
    gg2, gb2, gbo, gg1, gb1, gba, gbq, gbv, gbi = small
    half = D // 2
    kept = lax.dynamic_slice_in_dim(dx, sec * half, half, 2)
    sent = lax.dynamic_slice_in_dim(dx, (1 - sec) * half, half, 2).astype(BF)
    grad_input = jnp.where(first, kept, swapped(sent).astype(F32))[:, None]
    pooled_kept = lax.dynamic_slice_in_dim(pooled, sec * half, half, 2)
    pooled_sent = lax.dynamic_slice_in_dim(pooled, (1 - sec) * half, half, 2).astype(BF)
    pooled_out = jnp.where(first, swapped(pooled_sent).astype(F32), pooled_kept)
    loss_out = jnp.where(first, swapped(loss.astype(BF)).astype(F32), loss)
    return (pooled_out, loss_out, grad_input, g_qkv, gbq, gbv, g_at, gba, gg1, gb1, g_in, gbi, g_out, gbo, gg2, gb2)


def solution(mesh):
    in_specs = (
        P(None, "dp", None, None),
        P(None, "dp", None),
        P(None, "dp"),
        P("section", None, None),
        P("section", None),
        P("section", None),
        P("section", None, None),
        P("section", None),
        P("section", None),
        P("section", None),
        P("section", None, None),
        P("section", None),
        P("section", None, None),
        P("section", None),
        P("section", None),
        P("section", None),
    )
    out_specs = (
        P(None, "dp", "section"),
        P(None, "dp"),
        P(None, "dp", None, "section"),
        P("section", "dp", None),
        P("section", "dp"),
        P("section", "dp"),
        P("section", "dp", None),
        P("section", "dp"),
        P("section", "dp"),
        P("section", "dp"),
        P("section", "dp", None),
        P("section", "dp"),
        P("section", "dp", None),
        P("section", "dp"),
        P("section", "dp"),
        P("section", "dp"),
    )
    return jax.shard_map(local, mesh=mesh, in_specs=in_specs, out_specs=out_specs, check_vma=False)
```

time: 1520 us -> 593 us (0.39)
  waiting for transfers between devices: 824 us -> 180 us
  matrix products: 347 us -> 30.9 us
  Pallas kernels: 0 us -> 173 us
  local copies, waits for them, and re-layouts: 116 us -> 27.4 us
  other arithmetic: 112 us -> 56.2 us
  blocking collectives: 78.5 us -> 103 us
    reduce_scatter x4 -> x0, waiting for transfers between devices: 388 us -> none  [local(): lax.psum_scatter(tuple((grad_part[None] for grad_part in totals)), 'dp',...]
    dot_general x67 -> x7, matrix products: 347 us -> 30.9 us  [the longest x4 30.2 us: local(): jnp.einsum('mta,mtb->ab', a, b, preferred_element_type=F32).astype(BF)]
    unnamed x22 -> x2, waiting for transfers between devices: 404 us -> 180 us
    pallas_call x0 -> x2, Pallas kernels: none -> 173 us  [the longest x1 116 us: stack_bwd(): pl.pallas_call(functools.partial(bwd_kernel, tb, fc, kb), out_shape=out_s...]
    unnamed x0 -> x1, blocking collectives: none -> 62 us
    unnamed x444 -> x21, local copies, waits for them, and re-layouts: 47.2 us -> 3.75 us
    all_gather x4 -> x2, blocking collectives: 78.5 us -> 40.6 us  [the longest x1 23 us: contrast_head(): every = lax.all_gather(unit, 'dp', axis=1, tiled=True)]
    concatenate x0 -> x1, other arithmetic: none -> 37 us  [scattered(): packed = jnp.concatenate([g.reshape(count, -1) for g in grads], axis=1)]
  transfers between devices with their start and end apart: 20 -> 4, of which waited for: 15 -> 1; matrix products, arithmetic and copies ran while one was open for 11% -> 1% of each run, Pallas kernels for 0% -> 0%
where the time goes in v1:
time: 593 us; the launch traced here: 587 us
  waiting for transfers between devices  180 us (30%)
  Pallas kernels  173 us (29%)
  blocking collectives  103 us (17%)
  other arithmetic  56.2 us (9%)
  matrix products  30.9 us (5%)
  local copies, waits for them, and re-layouts  27.4 us (5%)
  between operations  14.6 us (2%)
    unnamed x2, waiting for transfers between devices  180 us
    pallas_call x1, Pallas kernels, stack_bwd(): pl.pallas_call(functools.partial(bwd_kernel, tb, fc, kb), out_shape=out_s...  116 us
    unnamed x1, blocking collectives  62 us
    pallas_call x1, Pallas kernels, stack_fwd(): pl.pallas_call(functools.partial(fwd_kernel, tb, fc, qb), out_shape=out_s...  57.2 us
    concatenate x1, other arithmetic, scattered(): packed = jnp.concatenate([g.reshape(count, -1) for g in grads], axis=1)  37 us
    dot_general x4, matrix products, local(): jnp.einsum('mta,mtb->ab', a, b, preferred_element_type=F32).astype(BF)  30.2 us
    all_gather x1, blocking collectives, contrast_head(): every = lax.all_gather(unit, 'dp', axis=1, tiled=True)  23 us
    all_gather x1, blocking collectives, local(): all_pairs = lax.all_gather(pair_ids, 'dp', axis=1, tiled=True)  17.6 us
  transfers between devices with their start and end apart: 4, of which 1 were waited for; matrix products, arithmetic and copies ran while one was open for 1% of the time, Pallas kernels for 0%

profile of v1, /device:TPU:0, one launch (start us, length us, event | category | flops | bytes accessed | tf_op | source)
XLA Modules:
  0.0 586.9 jit_solution(16069055826781548489)
XLA Ops:
  7.2 0.7 copy.87
  7.9 0.1 convert_reduce_fusion
  8.0 0.5 copy-done.4
  8.5 57.2 %stack_fwd.1 = (f32[2,16,768]{2,1,0:T(8,128)}, bf16[2,512,768]{2,1,0:T(8,128)(2,1)}, bf16[2,512,2304]{2,1,0:T(8,128)(2,1)}, f32[2,16,512]{2,1,0:T(8,128)}, bf16[...) custom-call(bf16[2,512,768]{2,1,0:T(8,128)(2,1)} %bitcast.43, ...), custom_call_target="tpu_custom_call" | custom-call | tf_op jit(solution)/shard_map/stack_fwd/pallas_call | solution.py:240
  65.7 1.0 multiply_reduce_fusion.1
  66.7 0.1 multiply_convert_fusion
  66.8 23.0 %all_gather.6 = bf16[2,64,768]{2,0,1:T(2,128)(2,1)S(1)} all-gather(bf16[2,4,768]{2,0,1:T(2,128)(2,1)S(1)} %copy.58), channel_id=1, replica_groups=mesh['section'=2,'dp'=16] {'dp'}, dimensions={1}, use_global_device_ids=true | all-gather | bytes 208896 | tf_op jit(solution)/shard_map/all_gather | solution.py:461
  89.8 17.6 %all-gather = s32[16,4,2]{1,2,0:T(2,128)S(1)} all-gather(s32[1,4,2]{1,2,0:T(2,128)S(1)} %bitcast.49), channel_id=1, replica_groups=mesh['section'=2,'dp'=16] {'dp'}, dimensions={0}, use_global_device_ids=true | all-gather | bytes 544 | tf_op jit(solution)/shard_map/all_gather | solution.py:504
  107.4 0.1 reshape.125
  107.5 0.2 fusion.17
  107.8 0.3 fusion.5
  108.1 0.2 multiply_reduce_fusion
  108.3 0.1 subtract_divide_fusion
  108.4 0.6 pad.4.dp
  109.0 115.7 %stack_bwd.1 = (f32[16,768]{1,0:T(8,128)}, f32[2,512,768]{2,1,0:T(8,128)}, bf16[2,512,768]{2,1,0:T(8,128)(2,1)}, bf16[2,512,3072]{2,1,0:T(8,128)(2,1)}, bf16[2,5...) custom-call(s32[2,512]{1,0:T(2,128)} %bitcast.46, f32[2,16,768]{2,1,0:T(8,128)} %pad.4.dp, ...), custom_call_target="tpu_custom_call" | custom-call | tf_op jit(solution)/shard_map/stack_bwd/pallas_call | solution.py:449
  224.7 9.2 %bitcast_convert_fusion = bf16[3072,768]{1,0:T(8,128)(2,1)} fusion(bf16[2,512,3072]{2,1,0:T(8,128)(2,1)} %get-tuple-element.49, bf16[2,512,768]{2,1,0:T(8,128)(2,1)} %get-tuple-element.50), kind=kOutput, calls=%fused_computation.1 | convolution fusion | flops 4834197504 | bytes 12582912 | tf_op jit(solution)/shard_map/mta,mtb->ab/dot_general | solution.py:508
  233.9 5.4 reshape.119
  239.2 9.7 %bitcast_convert_fusion.1 = bf16[768,3072]{1,0:T(8,128)(2,1)} fusion(bf16[2,512,768]{2,1,0:T(8,128)(2,1)S(1)} %copy-done.7, bf16[2,512,3072]{2,1,0:T(8,128)(2,1)} %get-tuple-element.48), kind=kOutput, calls=%fused_computation.2 | convolution fusion | flops 4834197504 | bytes 12582912 | tf_op jit(solution)/shard_map/mta,mtb->ab/dot_general | solution.py:508
  249.0 5.4 reshape.118
  254.3 2.8 bitcast_convert_fusion.3
  257.2 1.4 reshape.117
  258.6 8.5 %bitcast_convert_fusion.2 = bf16[768,2304]{1,0:T(8,128)(2,1)} fusion(bf16[2,512,768]{2,1,0:T(8,128)(2,1)} %get-tuple-element.44, bf16[2,512,2304]{2,1,0:T(8,128)(2,1)} %get-tuple-element.45), kind=kOutput, calls=%fused_computation.3 | convolution fusion | flops 3625648128 | bytes 9830400 | tf_op jit(solution)/shard_map/mta,mtb->ab/dot_general | solution.py:508
  267.0 3.1 reshape.116
  270.1 37.0 %pad_maximum_fusion = bf16[16,442368]{1,0:T(8,128)(2,1)} fusion(bf16[16,147456]{1,0:T(8,128)(2,1)} %reshape.119, bf16[16,147456]{1,0:T(8,128)(2,1)} %reshape.118, bf16[16,36864]{1,0:T(8,128)(2,1)} %reshape.117, bf16[16,110592]{1,0:T(8,128)(2,1)S(1)} %reshape.116), kind=kLoop, calls=%fused_computation | loop fusion | flops 56623104 | bytes 28311552 | tf_op jit(solution)/shard_map/concatenate | solution.py:484
  307.2 0.7 copy-done.3
  307.9 1.2 copy-done
  309.0 1.0 dynamic-slice_convert_fusion
  310.0 0.9 collective-permute-start.2
  310.9 1.2 collective-permute-start.1
  312.4 0.1 reshape_squeeze.27
  312.6 0.1 reshape_squeeze.30
  312.8 0.1 reshape_reshape.3
  312.9 0.6 dynamic-slice
  313.5 0.1 concatenate.7
  313.5 62.0 %all-reduce.2 = f32[16,576]{1,0:T(8,128)S(1)} all-reduce(f32[16,576]{1,0:T(8,128)S(1)} %concatenate.7), channel_id=3, replica_groups=mesh['section'=2,'dp'=16] {'dp'}, use_global_device_ids=true, to_apply=%region_7.8.clone | all-reduce | flops 9216 | bytes 73728
  375.6 1.3 dynamic-slice.12
  376.9 1.3 fusion.16
  378.1 0.6 convert_select_fusion
  378.8 0.6 dynamic-slice_select_fusion
  379.4 2.4 select_bitcast_fusion
  381.8 180.1 %all-reduce.5.cloned.1.call-done = bf16[16,442368]{1,0:T(8,128)(2,1)} async-done(((bf16[16,442368]{1,0:T(8,128)(2,1)}), bf16[16,442368]{1,0:T(8,128)(2,1)}) %all-reduce.5.cloned.1.call-update) | async-done | bytes 14155792
  561.9 3.5 fusion.3
  565.4 0.8 reshape.120
  566.2 2.2 fusion.8
  568.5 0.7 reshape.121
  569.1 8.6 %fusion.1 = (f32[147456]{0:T(1024)S(1)}, f32[147456]{0:T(1024)S(1)}) fusion(bf16[16,442368]{1,0:T(8,128)(2,1)} %all-reduce.5.cloned.1.call-done, u32[]{:T(128)} %bitcast.16, u32[]{:T(128)S(6)} %convert.16, u32[]{:T(128)S(6)} %convert.14), kind=kLoop, calls=%fused_computation.11 | loop fusion | flops 294912 | bytes 1769484 | tf_op jit(solution)/shard_map/slice | solution.py:489
  577.7 0.9 reshape.122
  578.6 0.9 reshape.123
  (39 shorter events, 0.8 us)
Async XLA Ops:
  7.2 554.7 %all-reduce.5.cloned.1.call-start = ((), (), s32[]{:S(2)}) async-start(), calls=%async_computation | async-start | bytes 28311552
  7.9 0.6 copy-start.4
  8.5 81.3 %copy-start.6 = (s32[2,4]{1,0:T(2,128)S(1)}, s32[2,4]{1,0:T(2,128)}, u32[]{:S(2)}) copy-start(s32[2,4]{1,0:T(2,128)} %param.18) | copy-start | bytes 100
  66.7 158.0 %copy-start.2 = (f32[2,4,768]{2,1,0:T(4,128)}, f32[2,4,768]{2,1,0:T(4,128)S(1)}, u32[]{:S(2)}) copy-start(f32[2,4,768]{2,1,0:T(4,128)S(1)} %get-tuple-element.129) | copy-start | bytes 73732
  233.9 5.4 copy-start.7
  249.0 5.4 copy-start.1
  307.1 0.7 copy-start.3
  307.1 1.9 copy-start
  307.1 5.0 copy-start.5
  307.1 5.7 copy-start.8
  307.9 70.9 %collective-permute-start = (bf16[2,4,384]{2,1,0:T(4,128)(2,1)S(1)}, bf16[2,4,384]{2,1,0:T(4,128)(2,1)S(1)}, u32[]{:S(2)}, u32[]{:S(2)}) collective-permute-start(bf16[2,4,384]{2,1,0:T(4,128)(2,1)S(1)} %dynamic-slice_convert_fusion.5), channel_id=1, source_target_pairs={{0,16},{16,0},{1,17},{17,1},{2,18},{18,2},{3,19},{19,3},{4,20},{20... | collective-permute-start | bytes 18440 | tf_op jit(solution)/shard_map/ppermute | solution.py:495
  310.0 69.4 %collective-permute-start.2 = (bf16[2,512,384]{2,1,0:T(8,128)(2,1)}, bf16[2,512,384]{2,1,0:T(8,128)(2,1)}, u32[]{:S(2)}, u32[]{:S(2)}) collective-permute-start(bf16[2,512,384]{2,1,0:T(8,128)(2,1)} %dynamic-slice_convert_fusion), channel_id=1, source_target_pairs={{0,16},{16,0},{1,17},{17,1},{2,18},{18,2},{3,19},{19,3},{4,20},{20... | collective-permute-start | bytes 2359304 | tf_op jit(solution)/shard_map/ppermute | solution.py:495
  310.9 67.2 %collective-permute-start.1 = (bf16[2,4]{1,0:T(2,128)(2,1)S(1)}, bf16[2,4]{1,0:T(2,128)(2,1)S(1)}, u32[]{:S(2)}, u32[]{:S(2)}) collective-permute-start(bf16[2,4]{1,0:T(2,128)(2,1)S(1)} %fusion.15), channel_id=1, source_target_pairs={{0,16},{16,0},{1,17},{17,1},{2,18},{18,2},{3,19},{19,3},{4,20},{20... | collective-permute-start | bytes 56 | tf_op jit(solution)/shard_map/ppermute | solution.py:495
Sparse Core Ops, SparseCore 0:
  307.3 254.5 all-reduce.4
